TPU v7x, 256 devices: a whole 4x4x8 slice. The times are simulated.
256 devices in a mesh: ab: 4 (over y), cd: 64 (over x, z, core).
Axes of the slice: x: 4, y: 4, z: 8, core: 2. Of those that a mesh axis runs over, the one named last changes fastest.
Arguments:
- ladder_ints: bfloat16 [8, 12288, 12288], P(None, 'cd', 'ab'), may hold values from -0.15625 to 0.15625
- amplitudes: bfloat16 [2048, 12288], P('ab', 'cd'), may hold values from -6 to 6
- group_sizes: int32 [8], replicated, may hold values from 1 to 768, 2048 in all
- occ_energy: float32 [2048], replicated, may hold values from -2.5 to -0.5
- vir_energy: float32 [8, 12288], replicated, may hold values from 0.5 to 6
Outputs:
- increment: bfloat16 [2048, 12288], P(None, ('ab', 'cd'))
Inputs may be any that keep to these rules, and one draw needn't show every extreme that they name: Group g holds the group_sizes[g] consecutive rows after those of groups 0 to g - 1; the sizes sum to 2048 and the largest is exactly 768.
All inputs are finite; a program needn't handle non-finite values.
Results may differ from a plain program's by a relative error of at most 0.0011.
Values may be sent and summed in bfloat16 or wider, within the bound.
No kernel may reach another device: no remote copies, remote signals or barrier semaphores. Data moves between devices by JAX's collectives and lax.ppermute only.
A program may use at most 192 MiB of HBM per device.

v0:
```python
import jax
import jax.numpy as jnp
from jax import lax
from jax.sharding import PartitionSpec as P

NIRREP = 8
BLOCK = 128


def grouped(amplitudes, ladder_ints, group_sizes):
    nrows = amplitudes.shape[0]
    width = ladder_ints.shape[2]
    ends = jnp.cumsum(group_sizes)
    starts = ends - group_sizes
    total = jnp.zeros((nrows, width), jnp.float32)
    for irrep in range(NIRREP):
        first = starts[irrep]
        count = group_sizes[irrep]
        blocks = (count + BLOCK - 1) // BLOCK
        table = ladder_ints[irrep]

        def step(index, acc, first=first, count=count, table=table):
            nominal = first + index * BLOCK
            begin = jnp.minimum(nominal, nrows - BLOCK)
            rows = lax.dynamic_slice_in_dim(amplitudes, begin, BLOCK, 0)
            ids = begin + jnp.arange(BLOCK, dtype=jnp.int32)
            keep = (ids >= nominal) & (ids < first + count)
            prod = jnp.dot(rows, table, preferred_element_type=jnp.float32)
            prod = jnp.where(keep[:, None], prod, jnp.zeros_like(prod))
            current = lax.dynamic_slice_in_dim(acc, begin, BLOCK, 0)
            return lax.dynamic_update_slice_in_dim(acc, current + prod, begin, 0)

        total = lax.fori_loop(0, blocks, step, total)
    return total


def scaled(partial_value, row_ids, ends, occ_rows, vir_cols):
    irreps = jnp.sum((row_ids[:, None] >= ends[None, :]).astype(jnp.int32), axis=1)
    onehot = (irreps[:, None] == jnp.arange(NIRREP, dtype=jnp.int32)[None, :]).astype(jnp.float32)
    vir_rows = jnp.sum(onehot[:, :, None] * vir_cols[None, :, :], axis=1)
    return (partial_value / (occ_rows[:, None] - vir_rows)).astype(jnp.bfloat16)


def body(ladder_ints, amplitudes, group_sizes, occ_energy, vir_energy):
    whole_rows = lax.all_gather(amplitudes, "ab", axis=0, tiled=True)
    ladder = grouped(whole_rows, ladder_ints, group_sizes)
    ab_width = ladder_ints.shape[2]
    ends = jnp.cumsum(group_sizes)
    ab_start = lax.axis_index("ab") * ab_width
    partial_value = lax.psum_scatter(ladder, "cd", scatter_dimension=0, tiled=True)
    local_rows = partial_value.shape[0]
    row_start = lax.axis_index("cd") * local_rows
    row_ids = row_start + jnp.arange(local_rows, dtype=jnp.int32)
    occ_rows = lax.dynamic_slice_in_dim(occ_energy, row_start, local_rows, 0)
    vir_cols = lax.dynamic_slice_in_dim(vir_energy, ab_start, ab_width, 1)
    result = scaled(partial_value, row_ids, ends, occ_rows, vir_cols)
    return lax.all_to_all(result, "cd", split_axis=1, concat_axis=0, tiled=True)


def solution(mesh):
    placed = (P(None, "cd", "ab"), P("ab", "cd"), P(), P(), P())
    return jax.shard_map(
        body, mesh=mesh, in_specs=placed, out_specs=P(None, ("ab", "cd")), check_vma=False
    )
```

profile of v0, /device:TPU:1, one launch (start us, length us, event | category | flops | bytes accessed | tf_op | source)
XLA Modules:
  0.0 458.6 jit_solution(12858130740716400737)
XLA Ops:
  16.4 6.9 %slice_bitcast_fusion = (bf16[192,3072]{1,0:T(8,128)(2,1)S(1)}, bf16[192,3072]{1,0:T(8,128)(2,1)}, bf16[192,3072]{1,0:T(8,128)(2,1)}, bf16[192,3072]{1,0:T(8,128...) fusion(bf16[8,192,3072]{2,1,0:T(8,128)(2,1)} %param.21), kind=kLoop, calls=%fused_computation.41 | loop fusion | bytes 18874368 | tf_op jit(solution)/shard_map/squeeze | solution.py:20
  23.4 14.7 %all_gather.3 = bf16[2048,192]{1,0:T(8,128)(2,1)} all-gather(bf16[512,192]{1,0:T(8,128)(2,1)S(1)} %copy.13), channel_id=1, replica_groups=mesh['ab'=4,'cd'=64] {'ab'}, dimensions={0}, use_global_device_ids=true | all-gather | bytes 983040 | tf_op jit(solution)/shard_map/all_gather | solution.py:45
  38.1 11.5 %broadcast_in_dim.85 = f32[2048,3072]{1,0:T(8,128)} broadcast(f32[]{:T(128)} %constant.295.clone.1), dimensions={} | broadcast | bytes 25165828 | tf_op jit(solution)/shard_map/broadcast_in_dim | solution.py:15
  49.6 15.3 %while.96 = (s32[]{:T(128)}, f32[2048,3072]{1,0:T(8,128)}, s32[]{:T(128)}, s32[]{:T(128)}, s32[]{:T(128)}, /*index=5*/bf16[2048,192]{1,0:T(8,128)(2,1)}, bf16[19...) while((s32[]{:T(128)}, f32[2048,3072]{1,0:T(8,128)}, s32[]{:T(128)}, ...), condition=%wide.region_2.3_spmd, body=%wide.region_1.2_spmd.sunk | while | flops 151781888 | bytes 7538123 | solution.py:33
  50.2 2.3 fusion.61
  52.5 4.8 %dynamic_update_slice.48 = f32[2048,3072]{1,0:T(8,128)} dynamic-update-slice(f32[2048,3072]{1,0:T(8,128)} %get-tuple-element.1210, f32[128,3072]{1,0:T(8,128)S(1)} %fusion.61, s32[]{:T(128)S(6)} %select_n.180, s32[]{:T(128)} %constant.294.clone.1..sunk) | dynamic-update-slice | bytes 3145732 | tf_op jit(solution)/shard_map/while/body/dynamic_update_slice | solution.py:31
  57.9 2.2 fusion.61
  60.1 4.8 %dynamic_update_slice.48 = f32[2048,3072]{1,0:T(8,128)} dynamic-update-slice(f32[2048,3072]{1,0:T(8,128)} %get-tuple-element.1210, f32[128,3072]{1,0:T(8,128)S(1)} %fusion.61, s32[]{:T(128)S(6)} %select_n.180, s32[]{:T(128)} %constant.294.clone.1..sunk) | dynamic-update-slice | bytes 3145732 | tf_op jit(solution)/shard_map/while/body/dynamic_update_slice | solution.py:31
  66.2 7.7 %while.97 = (s32[]{:T(128)}, f32[2048,3072]{1,0:T(8,128)}, s32[]{:T(128)}, s32[]{:T(128)}, s32[]{:T(128)}, /*index=5*/bf16[2048,192]{1,0:T(8,128)(2,1)}, bf16[19...) while((s32[]{:T(128)}, f32[2048,3072]{1,0:T(8,128)}, s32[]{:T(128)}, ...), condition=%wide.region_4.5_spmd, body=%wide.region_3.4_spmd.sunk | while | flops 151781888 | bytes 7538123 | solution.py:33
  66.9 2.2 fusion.64
  69.1 4.8 %dynamic_update_slice.49 = f32[2048,3072]{1,0:T(8,128)} dynamic-update-slice(f32[2048,3072]{1,0:T(8,128)} %get-tuple-element.1246, f32[128,3072]{1,0:T(8,128)S(1)} %fusion.64, s32[]{:T(128)S(6)} %select_n.182, s32[]{:T(128)} %constant.294.clone.1..sunk.1) | dynamic-update-slice | bytes 3145732 | tf_op jit(solution)/shard_map/while/body/dynamic_update_slice | solution.py:31
  75.2 46.6 %while.98 = (s32[]{:T(128)}, f32[2048,3072]{1,0:T(8,128)}, s32[]{:T(128)}, s32[]{:T(128)}, s32[]{:T(128)}, /*index=5*/bf16[2048,192]{1,0:T(8,128)(2,1)}, bf16[19...) while((s32[]{:T(128)}, f32[2048,3072]{1,0:T(8,128)}, s32[]{:T(128)}, ...), condition=%wide.region_6.7_spmd, body=%wide.region_5.6_spmd.sunk | while | flops 151781888 | bytes 7538123 | solution.py:33
  75.9 2.3 fusion.67
  78.2 4.8 %dynamic_update_slice.50 = f32[2048,3072]{1,0:T(8,128)} dynamic-update-slice(f32[2048,3072]{1,0:T(8,128)} %get-tuple-element.1282, f32[128,3072]{1,0:T(8,128)S(1)} %fusion.67, s32[]{:T(128)S(6)} %select_n.184, s32[]{:T(128)} %constant.294.clone.1..sunk.2) | dynamic-update-slice | bytes 3145732 | tf_op jit(solution)/shard_map/while/body/dynamic_update_slice | solution.py:31
  85.9 4.8 %dynamic_update_slice.50 = f32[2048,3072]{1,0:T(8,128)} dynamic-update-slice(f32[2048,3072]{1,0:T(8,128)} %get-tuple-element.1282, f32[128,3072]{1,0:T(8,128)S(1)} %fusion.67, s32[]{:T(128)S(6)} %select_n.184, s32[]{:T(128)} %constant.294.clone.1..sunk.2) | dynamic-update-slice | bytes 3145732 | tf_op jit(solution)/shard_map/while/body/dynamic_update_slice | solution.py:31
  91.4 2.3 fusion.67
  93.7 4.8 %dynamic_update_slice.50 = f32[2048,3072]{1,0:T(8,128)} dynamic-update-slice(f32[2048,3072]{1,0:T(8,128)} %get-tuple-element.1282, f32[128,3072]{1,0:T(8,128)S(1)} %fusion.67, s32[]{:T(128)S(6)} %select_n.184, s32[]{:T(128)} %constant.294.clone.1..sunk.2) | dynamic-update-slice | bytes 3145732 | tf_op jit(solution)/shard_map/while/body/dynamic_update_slice | solution.py:31
  99.2 2.3 fusion.67
  101.4 4.8 %dynamic_update_slice.50 = f32[2048,3072]{1,0:T(8,128)} dynamic-update-slice(f32[2048,3072]{1,0:T(8,128)} %get-tuple-element.1282, f32[128,3072]{1,0:T(8,128)S(1)} %fusion.67, s32[]{:T(128)S(6)} %select_n.184, s32[]{:T(128)} %constant.294.clone.1..sunk.2) | dynamic-update-slice | bytes 3145732 | tf_op jit(solution)/shard_map/while/body/dynamic_update_slice | solution.py:31
  107.0 2.3 fusion.67
  109.2 4.8 %dynamic_update_slice.50 = f32[2048,3072]{1,0:T(8,128)} dynamic-update-slice(f32[2048,3072]{1,0:T(8,128)} %get-tuple-element.1282, f32[128,3072]{1,0:T(8,128)S(1)} %fusion.67, s32[]{:T(128)S(6)} %select_n.184, s32[]{:T(128)} %constant.294.clone.1..sunk.2) | dynamic-update-slice | bytes 3145732 | tf_op jit(solution)/shard_map/while/body/dynamic_update_slice | solution.py:31
  114.7 2.2 fusion.67
  117.0 4.8 %dynamic_update_slice.50 = f32[2048,3072]{1,0:T(8,128)} dynamic-update-slice(f32[2048,3072]{1,0:T(8,128)} %get-tuple-element.1282, f32[128,3072]{1,0:T(8,128)S(1)} %fusion.67, s32[]{:T(128)S(6)} %select_n.184, s32[]{:T(128)} %constant.294.clone.1..sunk.2) | dynamic-update-slice | bytes 3145732 | tf_op jit(solution)/shard_map/while/body/dynamic_update_slice | solution.py:31
  123.0 30.5 %while.99 = (s32[]{:T(128)}, f32[2048,3072]{1,0:T(8,128)}, s32[]{:T(128)}, s32[]{:T(128)}, s32[]{:T(128)}, /*index=5*/bf16[2048,192]{1,0:T(8,128)(2,1)}, bf16[19...) while((s32[]{:T(128)}, f32[2048,3072]{1,0:T(8,128)}, s32[]{:T(128)}, ...), condition=%wide.region_8.9_spmd, body=%wide.region_7.8_spmd.sunk | while | flops 151781888 | bytes 7538123 | solution.py:33
  123.6 2.3 fusion.70
  125.8 4.8 %dynamic_update_slice.51 = f32[2048,3072]{1,0:T(8,128)} dynamic-update-slice(f32[2048,3072]{1,0:T(8,128)} %get-tuple-element.1318, f32[128,3072]{1,0:T(8,128)S(1)} %fusion.70, s32[]{:T(128)S(6)} %select_n.186, s32[]{:T(128)} %constant.294.clone.1..sunk.3) | dynamic-update-slice | bytes 3145732 | tf_op jit(solution)/shard_map/while/body/dynamic_update_slice | solution.py:31
  131.2 2.3 fusion.70
  133.5 4.8 %dynamic_update_slice.51 = f32[2048,3072]{1,0:T(8,128)} dynamic-update-slice(f32[2048,3072]{1,0:T(8,128)} %get-tuple-element.1318, f32[128,3072]{1,0:T(8,128)S(1)} %fusion.70, s32[]{:T(128)S(6)} %select_n.186, s32[]{:T(128)} %constant.294.clone.1..sunk.3) | dynamic-update-slice | bytes 3145732 | tf_op jit(solution)/shard_map/while/body/dynamic_update_slice | solution.py:31
  138.8 2.2 fusion.70
  141.1 4.8 %dynamic_update_slice.51 = f32[2048,3072]{1,0:T(8,128)} dynamic-update-slice(f32[2048,3072]{1,0:T(8,128)} %get-tuple-element.1318, f32[128,3072]{1,0:T(8,128)S(1)} %fusion.70, s32[]{:T(128)S(6)} %select_n.186, s32[]{:T(128)} %constant.294.clone.1..sunk.3) | dynamic-update-slice | bytes 3145732 | tf_op jit(solution)/shard_map/while/body/dynamic_update_slice | solution.py:31
  146.5 2.2 fusion.70
  148.7 4.8 %dynamic_update_slice.51 = f32[2048,3072]{1,0:T(8,128)} dynamic-update-slice(f32[2048,3072]{1,0:T(8,128)} %get-tuple-element.1318, f32[128,3072]{1,0:T(8,128)S(1)} %fusion.70, s32[]{:T(128)S(6)} %select_n.186, s32[]{:T(128)} %constant.294.clone.1..sunk.3) | dynamic-update-slice | bytes 3145732 | tf_op jit(solution)/shard_map/while/body/dynamic_update_slice | solution.py:31
  154.7 15.4 %while.100 = (s32[]{:T(128)}, f32[2048,3072]{1,0:T(8,128)}, s32[]{:T(128)}, s32[]{:T(128)}, s32[]{:T(128)}, /*index=5*/bf16[2048,192]{1,0:T(8,128)(2,1)}, bf16[1...) while((s32[]{:T(128)}, f32[2048,3072]{1,0:T(8,128)}, ...), condition=%wide.region_10.11_spmd, body=%wide.region_9.10_spmd.sunk | while | flops 151781888 | bytes 7538123 | solution.py:33
  155.3 2.3 fusion.73
  157.6 4.8 %dynamic_update_slice.52 = f32[2048,3072]{1,0:T(8,128)} dynamic-update-slice(f32[2048,3072]{1,0:T(8,128)} %get-tuple-element.1354, f32[128,3072]{1,0:T(8,128)S(1)} %fusion.73, s32[]{:T(128)S(6)} %select_n.188, s32[]{:T(128)} %constant.294.clone.1..sunk.4) | dynamic-update-slice | bytes 3145732 | tf_op jit(solution)/shard_map/while/body/dynamic_update_slice | solution.py:31
  163.0 2.3 fusion.73
  165.3 4.8 %dynamic_update_slice.52 = f32[2048,3072]{1,0:T(8,128)} dynamic-update-slice(f32[2048,3072]{1,0:T(8,128)} %get-tuple-element.1354, f32[128,3072]{1,0:T(8,128)S(1)} %fusion.73, s32[]{:T(128)S(6)} %select_n.188, s32[]{:T(128)} %constant.294.clone.1..sunk.4) | dynamic-update-slice | bytes 3145732 | tf_op jit(solution)/shard_map/while/body/dynamic_update_slice | solution.py:31
  171.3 7.7 %while.101 = (s32[]{:T(128)}, f32[2048,3072]{1,0:T(8,128)}, s32[]{:T(128)}, s32[]{:T(128)}, s32[]{:T(128)}, /*index=5*/bf16[2048,192]{1,0:T(8,128)(2,1)}, bf16[1...) while((s32[]{:T(128)}, f32[2048,3072]{1,0:T(8,128)}, ...), condition=%wide.region_12.13_spmd, body=%wide.region_11.12_spmd.sunk | while | flops 151781888 | bytes 7538123 | solution.py:33
  171.9 2.2 fusion.76
  174.2 4.8 %dynamic_update_slice.53 = f32[2048,3072]{1,0:T(8,128)} dynamic-update-slice(f32[2048,3072]{1,0:T(8,128)} %get-tuple-element.1390, f32[128,3072]{1,0:T(8,128)S(1)} %fusion.76, s32[]{:T(128)S(6)} %select_n.190, s32[]{:T(128)} %constant.294.clone.1..sunk.5) | dynamic-update-slice | bytes 3145732 | tf_op jit(solution)/shard_map/while/body/dynamic_update_slice | solution.py:31
  180.3 15.2 %while.102 = (s32[]{:T(128)}, f32[2048,3072]{1,0:T(8,128)}, s32[]{:T(128)}, s32[]{:T(128)}, s32[]{:T(128)}, /*index=5*/bf16[2048,192]{1,0:T(8,128)(2,1)}, bf16[1...) while((s32[]{:T(128)}, f32[2048,3072]{1,0:T(8,128)}, ...), condition=%wide.region_14.15_spmd, body=%wide.region_13.14_spmd.sunk | while | flops 151781888 | bytes 7538123 | solution.py:33
  180.9 2.2 fusion.79
  183.2 4.8 %dynamic_update_slice.54 = f32[2048,3072]{1,0:T(8,128)} dynamic-update-slice(f32[2048,3072]{1,0:T(8,128)} %get-tuple-element.1426, f32[128,3072]{1,0:T(8,128)S(1)} %fusion.79, s32[]{:T(128)S(6)} %select_n.192, s32[]{:T(128)} %constant.294.clone.1..sunk.6) | dynamic-update-slice | bytes 3145732 | tf_op jit(solution)/shard_map/while/body/dynamic_update_slice | solution.py:31
  190.9 4.6 %dynamic_update_slice.54 = f32[2048,3072]{1,0:T(8,128)} dynamic-update-slice(f32[2048,3072]{1,0:T(8,128)} %get-tuple-element.1426, f32[128,3072]{1,0:T(8,128)S(1)} %fusion.79, s32[]{:T(128)S(6)} %select_n.192, s32[]{:T(128)} %constant.294.clone.1..sunk.6) | dynamic-update-slice | bytes 3145732 | tf_op jit(solution)/shard_map/while/body/dynamic_update_slice | solution.py:31
  196.6 7.1 %while.103 = (s32[]{:T(128)}, f32[2048,3072]{1,0:T(8,128)}, s32[]{:T(128)}, s32[]{:T(128)}, s32[]{:T(128)}, /*index=5*/bf16[2048,192]{1,0:T(8,128)(2,1)}, bf16[1...) while((s32[]{:T(128)}, f32[2048,3072]{1,0:T(8,128)}, ...), condition=%wide.region_16.17_spmd, body=%wide.region_15.16_spmd.sunk | while | flops 151781888 | bytes 7538123 | solution.py:33
  199.1 4.6 %dynamic_update_slice.55 = f32[2048,3072]{1,0:T(8,128)} dynamic-update-slice(f32[2048,3072]{1,0:T(8,128)} %get-tuple-element.1462, f32[128,3072]{1,0:T(8,128)S(1)} %fusion.82, s32[]{:T(128)S(6)} %select_n.194, s32[]{:T(128)} %constant.294.clone.1..sunk.7) | dynamic-update-slice | bytes 3145732 | tf_op jit(solution)/shard_map/while/body/dynamic_update_slice | solution.py:31
  206.0 218.9 %reduce-scatter.2.cloned.1.call-done = f32[32,3072]{1,0:T(8,128)} async-done(((f32[2048,3072]{1,0:T(8,128)}), f32[32,3072]{1,0:T(8,128)}) %reduce-scatter.2.cloned.1.call-update) | async-done | bytes 393232 | tf_op jit(solution)/shard_map/reduce_scatter | solution.py:50
  427.7 22.7 %all_to_all.19 = bf16[64,2,768]{2,1,0:T(2,128)(2,1)S(1)} all-to-all(bf16[64,2,768]{2,1,0:T(2,128)(2,1)S(1)} %reshape.112), channel_id=1, replica_groups=mesh['ab'=4,'cd'=64] {'cd'}, dimensions={0} | all-to-all | bytes 393216 | tf_op jit(solution)/shard_map/all_to_all | solution.py:57
  (45 shorter events, 16.8 us)
Async XLA Ops:
  6.5 198.2 %copy-start = (f32[8,12288]{1,0:T(8,128)S(1)}, f32[8,12288]{1,0:T(8,128)}, u32[]{:S(2)}) copy-start(f32[8,12288]{1,0:T(8,128)} %param.25) | copy-start | bytes 1179652
  6.5 418.4 %reduce-scatter.2.cloned.1.call-start = ((), (), s32[]{:S(2)}) async-start(), calls=%async_computation.2 | async-start | bytes 25559040 | tf_op jit(solution)/shard_map/reduce_scatter | solution.py:50
  16.4 6.9 %copy-start.1 = (bf16[512,192]{0,1:T(8,128)(2,1)S(1)}, bf16[512,192]{0,1:T(8,128)(2,1)}, u32[]{:S(2)}) copy-start(bf16[512,192]{0,1:T(8,128)(2,1)} %param.22) | copy-start | bytes 589828
Sparse Core Ops, SparseCore 0:
  203.9 221.0 reduce-scatter.1
where the time goes:
time: 462 us; the launch traced here: 459 us
  waiting for transfers between devices  219 us (47%)
  local copies, waits for them, and re-layouts  115 us (25%)
  matrix products  42.3 us (9%)
  blocking collectives  37.4 us (8%)
  between operations  28.2 us (6%)
  loops' own time  12.6 us (3%)
    reduce_scatter x1, waiting for transfers between devices, body(): lax.psum_scatter(ladder, 'cd', scatter_dimension=0, tiled=True)  219 us
    dynamic_update_slice x19, local copies, waits for them, and re-layouts, step(): return lax.dynamic_update_slice_in_dim(acc, current + prod, begin, 0)  90.4 us
    dot_general x19, matrix products, step(): prod = jnp.dot(rows, table, preferred_element_type=jnp.float32)  42.3 us
    all_to_all x1, blocking collectives, body(): return lax.all_to_all(result, 'cd', split_axis=1, concat_axis=0, tiled=True)  22.7 us
    all_gather x1, blocking collectives, body(): whole_rows = lax.all_gather(amplitudes, 'ab', axis=0, tiled=True)  14.7 us
    another operation x8, loops' own time, grouped(): total = lax.fori_loop(0, blocks, step, total)  12.6 us
    broadcast_in_dim x1, local copies, waits for them, and re-layouts, grouped(): total = jnp.zeros((nrows, width), jnp.float32)  11.5 us
  transfers between devices with their start and end apart: 1, of which 1 were waited for; matrix products, arithmetic and copies ran while one was open for 0% of the time, Pallas kernels for 0%

commit v1 on v0

v1 whole, which is shorter than its diff:
```python
import functools

import jax
import jax.numpy as jnp
from jax import lax
from jax.experimental import pallas as pl
from jax.experimental.pallas import tpu as pltpu
from jax.sharding import PartitionSpec as P

NIRREP = 8
NX, NZ, NC = 4, 8, 2
UNIT = 48
TILE = 128
WIDE = 384
PEAK = 32700.0
STEPS = 128.0
ROUND = 12582912.0
LEAST = 2.0**-100


def permutation(dx, dz, dc):
    def at(x, z, c):
        return ((x % NX) * NZ + z % NZ) * NC + c % NC

    return [
        (at(x, z, c), at(x + dx, z + dz, c + dc))
        for x in range(NX)
        for z in range(NZ)
        for c in range(NC)
    ]


def shifted(value, dx, dz, dc):
    return lax.ppermute(value, "cd", permutation(dx, dz, dc))


def ladder_kernel(offset, meta, sizes, t0_ref, t1_ref, v0_ref, v1_ref, out_ref, acc_ref):
    rows = acc_ref.shape[0]
    base = meta[2] * (2 * rows) + offset
    acc_ref[...] = jnp.zeros_like(acc_ref)
    first = jnp.int32(0)
    for g in range(NIRREP):
        last = first + sizes[g]
        low = jnp.clip(first - base, 0, rows)
        high = jnp.clip(last - base, 0, rows)

        def tile(t, carry, g=g, low=low, high=high):
            at = pl.multiple_of(t * TILE, TILE)
            prod = jnp.dot(t0_ref[pl.ds(at, TILE), :], v0_ref[g], preferred_element_type=jnp.float32)
            prod += jnp.dot(t1_ref[pl.ds(at, TILE), :], v1_ref[g], preferred_element_type=jnp.float32)
            ids = at + lax.broadcasted_iota(jnp.int32, prod.shape, 0)
            keep = (ids >= low) & (ids < high)
            acc_ref[pl.ds(at, TILE), :] += jnp.where(keep, prod, 0.0)
            return carry

        begin = low >> 7
        lax.fori_loop(begin, jnp.where(high > low, (high + TILE - 1) >> 7, begin), tile, 0)
        first = last
    for t in range(rows // TILE):
        out_ref[:, t * TILE : (t + 1) * TILE] = acc_ref[t * TILE : (t + 1) * TILE, :].T


def ladder(meta, sizes, t0, t1, v0, v1, offset, rows):
    depth, width = v0.shape[1:]
    part = offset // rows
    spec_t = pl.BlockSpec((rows, depth), lambda i, *_: (part, 0))
    spec_v = pl.BlockSpec((NIRREP, depth, WIDE), lambda i, *_: (0, 0, i))
    return pl.pallas_call(
        functools.partial(ladder_kernel, offset),
        out_shape=jax.ShapeDtypeStruct((width, rows), jnp.float32),
        grid_spec=pltpu.PrefetchScalarGridSpec(
            num_scalar_prefetch=2,
            grid=(width // WIDE,),
            in_specs=[spec_t, spec_t, spec_v, spec_v],
            out_specs=pl.BlockSpec((WIDE, rows), lambda i, *_: (i, 0)),
            scratch_shapes=[pltpu.VMEM((rows, WIDE), jnp.float32)],
        ),
        compiler_params=pltpu.CompilerParams(vmem_limit_bytes=40 << 20),
        cost_estimate=pl.CostEstimate(
            flops=4 * rows * depth * width * 2, bytes_accessed=30 << 20, transcendentals=0
        ),
        name="ladder",
    )(meta, sizes, t0, t1, v0, v1)


def scale_of(code):
    return jnp.exp2(code * (1.0 / STEPS)) * (1.0 / PEAK)


def decode_scales(message_ref, scales_ref):
    n = message_ref.shape[0] // UNIT
    scales_ref[...] = scale_of(message_ref[n * UNIT : n * UNIT + 16, :].astype(jnp.float32))


def received(message_ref, scales_ref, unit):
    at = jnp.maximum(unit, 0)
    factor = jnp.where(unit >= 0, 1.0, 0.0)
    values = message_ref[pl.ds(pl.multiple_of(at * UNIT, 16), UNIT), :].astype(jnp.float32)
    return values * (scales_ref[pl.ds(at, 1), :] * factor)


def hop_kernel(n, group, units, n_msgs, meta, *refs):
    own_refs, refs = refs[:2], refs[2:]
    msg_refs, refs = refs[:n_msgs], refs[n_msgs:]
    out_refs, refs = refs[:2], refs[2:]
    code_refs, scale_refs = refs[:2], refs[2:]
    step = pl.program_id(0)

    @pl.when(step == 0)
    def _():
        for m, s in zip(msg_refs, scale_refs):
            decode_scales(m, s)
        for c in code_refs:
            c[...] = jnp.zeros_like(c)

    for d in range(2):
        for k in range(group):
            i = step * group + k
            value = own_refs[d][k * UNIT : (k + 1) * UNIT, :]
            for j, unit in units(d, i, meta):
                value = value + received(msg_refs[j], scale_refs[j], unit)
            most = jnp.maximum(jnp.max(jnp.abs(value), axis=0, keepdims=True), LEAST)
            code = jnp.floor(jnp.log2(most) * STEPS) + 2.0
            coded = value * (1.0 / scale_of(code))
            coded = (coded + ROUND) - ROUND
            rows = pl.ds(pl.multiple_of(i * UNIT, 16), UNIT)
            out_refs[d][rows, :] = coded.astype(jnp.int32).astype(jnp.int16)
            code_refs[d][pl.ds(i, 1), :] = code

    @pl.when(step == n // group - 1)
    def _():
        for d in range(2):
            codes = code_refs[d][...].astype(jnp.int32).astype(jnp.int16)
            out_refs[d][n * UNIT : n * UNIT + 16, :] = codes


def hop(meta, own, msgs, n, group, block, units):
    rows = own.shape[1]

    def own_spec(d):
        return pl.BlockSpec((group * UNIT, rows), lambda s, meta: (block(d, s, meta), 0))

    def whole(shape):
        return pl.BlockSpec(shape, lambda s, meta: (0, 0))

    shape = (n * UNIT + 16, rows)
    return pl.pallas_call(
        functools.partial(hop_kernel, n, group, units, len(msgs)),
        out_shape=[jax.ShapeDtypeStruct(shape, jnp.int16)] * 2,
        grid_spec=pltpu.PrefetchScalarGridSpec(
            num_scalar_prefetch=1,
            grid=(n // group,),
            in_specs=[own_spec(0), own_spec(1)] + [whole(m.shape) for m in msgs],
            out_specs=[whole(shape)] * 2,
            scratch_shapes=[pltpu.VMEM((16, rows), jnp.float32)] * (2 + len(msgs)),
        ),
        compiler_params=pltpu.CompilerParams(vmem_limit_bytes=40 << 20),
        cost_estimate=pl.CostEstimate(
            flops=20 * n * UNIT * rows, bytes_accessed=16 * n * UNIT * rows, transcendentals=0
        ),
        name="hop",
    )(meta, own, own, *msgs)


def both_ways(pair, axis):
    dx, dz = (1, 0) if axis == "x" else (0, 1)
    return [shifted(pair[0], dx, dz, 0), shifted(pair[1], -dx, -dz, 0)]


def ring(meta, own, before, axis, count, unit_of, block_of):
    size, here = (NX, 0) if axis == "x" else (NZ, 1)
    sign = (1, -1)
    kept = len(before)
    moving = []
    for step in range(size // 2):
        ahead = size // 2 - step
        halved = step == 0
        n = count // 2 if halved else count
        group = min(4 if count == 16 else 2, n)

        def place(d, meta, ahead=ahead):
            return (meta[here] + sign[d] * ahead + size) & (size - 1)

        def block(d, s, meta, group=group, halved=halved, place=place):
            skip = d * (count // 2 // group) if halved else 0
            return block_of(place(d, meta), group, s + skip, meta)

        def units(d, i, meta, step=step, halved=halved, place=place):
            at = i + d * (count // 2) if halved else i
            found = [(j, unit_of(place(d, meta), at)) for j in range(kept)]
            if step == 1:
                half = count // 2
                found.append((kept + d, jnp.where(i < half, i, -1) if d == 0 else jnp.where(i >= half, i - half, -1)))
            elif step > 1:
                found.append((kept + d, i))
            return found

        moving = both_ways(hop(meta, own, before + moving, n, group, block, units), axis)
    return moving


def last_kernel(n_parts, meta, sizes, *refs):
    own_refs, refs = refs[:n_parts], refs[n_parts:]
    msg_refs, refs = refs[: 4 * n_parts], refs[4 * n_parts :]
    occ_ref, vir_ref, mine_ref, other_ref = refs[:4]
    scale_refs = refs[4:]
    x, z, core = meta[0], meta[1], meta[2]
    rows = own_refs[0].shape[1]
    for m, s in zip(msg_refs, scale_refs):
        decode_scales(m, s)
    for p in range(n_parts):
        ids = core * (n_parts * rows) + p * rows + lax.broadcasted_iota(jnp.int32, (1, rows), 1)
        for out_ref, c in ((mine_ref, core), (other_ref, 1 - core)):
            at = pl.ds(pl.multiple_of(c * UNIT, 16), UNIT)
            total = own_refs[p][at, :]
            before = (2 * z if p == 0 else 2 * x) + c
            for j, unit in enumerate((before, before, c, c)):
                total = total + received(msg_refs[4 * p + j], scale_refs[4 * p + j], unit)
            vir = jnp.zeros((UNIT, rows), jnp.float32)
            first = jnp.int32(0)
            for g in range(NIRREP):
                last = first + sizes[g]
                inside = jnp.where((ids >= first) & (ids < last), 1.0, 0.0)
                vir = vir + inside * vir_ref[at, g : g + 1]
                first = last
            cols = slice(p * rows, (p + 1) * rows)
            out_ref[:, cols] = (total / (occ_ref[:, cols] - vir)).astype(jnp.bfloat16)


def last(meta, sizes, owns, msgs, occ, vir):
    rows = owns[0].shape[1]

    def whole(shape):
        return pl.BlockSpec(shape, lambda s, meta, sizes: (0, 0))

    own_spec = pl.BlockSpec((2 * UNIT, rows), lambda s, meta, sizes: (meta[0] * NZ + meta[1], 0))
    shape = (UNIT, len(owns) * rows)
    return pl.pallas_call(
        functools.partial(last_kernel, len(owns)),
        out_shape=[jax.ShapeDtypeStruct(shape, jnp.bfloat16)] * 2,
        grid_spec=pltpu.PrefetchScalarGridSpec(
            num_scalar_prefetch=2,
            grid=(1,),
            in_specs=[own_spec] * len(owns) + [whole(m.shape) for m in msgs] + [whole(occ.shape), whole(vir.shape)],
            out_specs=[whole(shape)] * 2,
            scratch_shapes=[pltpu.VMEM((16, rows), jnp.float32)] * len(msgs),
        ),
        compiler_params=pltpu.CompilerParams(vmem_limit_bytes=40 << 20),
        name="last",
    )(meta, sizes, *owns, *msgs, occ, vir)


def body(ladder_ints, amplitudes, group_sizes, occ_energy, vir_energy):
    place = lax.axis_index("cd").astype(jnp.int32)
    x, z, core = place // (NZ * NC), (place // NC) % NZ, place % NC
    meta = jnp.stack([x, z, core]).astype(jnp.int32)
    their_ints = shifted(ladder_ints, 0, 0, 1)
    slab = lax.all_gather(amplitudes, "ab", axis=0, tiled=True)
    half = slab.shape[0] // 2
    my_rows = lax.dynamic_slice_in_dim(slab, core * half, half, 0)
    their_rows = lax.dynamic_slice_in_dim(slab, (1 - core) * half, half, 0)
    got_rows = shifted(their_rows, 0, 0, 1)
    rows = half // 2

    def product(offset):
        return ladder(meta, group_sizes, my_rows, got_rows, ladder_ints, their_ints, offset, rows)

    own_a = product(0)
    own_b = product(rows)

    def block_ax(p, group, s, meta):
        return p * (2 * NZ // group) + s

    def block_az(p, group, s, meta):
        return (meta[0] * NZ + p) * (2 // group) + s

    def block_bz(p, group, s, meta):
        return s * NZ + p

    def block_bx(p, group, s, meta):
        return (p * NZ + meta[1]) * (2 // group) + s

    def next_unit(p, i):
        return 2 * p + i

    ax = ring(meta, own_a, [], "x", 2 * NZ, None, block_ax)
    bz = ring(meta, own_b, [], "z", 2 * NX, None, block_bz)
    az = ring(meta, own_a, ax, "z", 2, next_unit, block_az)
    bx = ring(meta, own_b, bz, "x", 2, next_unit, block_bx)

    owner = lax.axis_index("ab") * ladder_ints.shape[2] + (place // NC) * (2 * UNIT)
    vir = lax.dynamic_slice_in_dim(vir_energy, owner, 2 * UNIT, 1).T
    occ = lax.dynamic_slice_in_dim(occ_energy, core * half, half, 0)[None, :]
    mine, other = last(meta, group_sizes, [own_a, own_b], ax + az + bz + bx, occ, vir)
    got = shifted(other, 0, 0, 1)
    low = jnp.where(core == 0, mine, got)
    high = jnp.where(core == 0, got, mine)
    return jnp.concatenate([low, high], axis=1).T


def solution(mesh):
    placed = (P(None, "cd", "ab"), P("ab", "cd"), P(), P(), P())
    return jax.shard_map(
        body, mesh=mesh, in_specs=placed, out_specs=P(None, ("ab", "cd")), check_vma=False
    )
```

time: 462 us -> 143 us (0.31)
  waiting for transfers between devices: 219 us -> 23.9 us
  local copies, waits for them, and re-layouts: 115 us -> 4.75 us
  starting transfers between devices: 0.01 us -> 55 us
  Pallas kernels: 0 us -> 44.9 us
  matrix products: 42.3 us -> 0 us
  between operations: 28.2 us -> 0.2 us
  blocking collectives: 37.4 us -> 13.3 us
  loops' own time: 12.6 us -> 0 us
    reduce_scatter x1 -> x0, waiting for transfers between devices: 219 us -> none  [body(): lax.psum_scatter(ladder, 'cd', scatter_dimension=0, tiled=True)]
    dynamic_update_slice x19 -> x0, local copies, waits for them, and re-layouts: 90.4 us -> none  [step(): return lax.dynamic_update_slice_in_dim(acc, current + prod, begin, 0)]
    ppermute x0 -> x27, starting transfers between devices: none -> 55 us  [shifted(): return lax.ppermute(value, 'cd', permutation(dx, dz, dc))]
    pallas_call x0 -> x15, Pallas kernels: none -> 44.9 us  [the longest x2 28.5 us: ladder(): pl.pallas_call(functools.partial(ladder_kernel, offset), out_shape=jax.Sh...]
    dot_general x19 -> x0, matrix products: 42.3 us -> none  [step(): prod = jnp.dot(rows, table, preferred_element_type=jnp.float32)]
    ppermute x0 -> x27, waiting for transfers between devices: none -> 23.9 us  [shifted(): return lax.ppermute(value, 'cd', permutation(dx, dz, dc))]
    all_to_all x1 -> x0, blocking collectives: 22.7 us -> none  [body(): return lax.all_to_all(result, 'cd', split_axis=1, concat_axis=0, tiled=True)]
    another operation x8 -> x0, loops' own time: 12.6 us -> none  [grouped(): total = lax.fori_loop(0, blocks, step, total)]
  transfers between devices with their start and end apart: 1 -> 27, of which waited for: 1 -> 9; matrix products, arithmetic and copies ran while one was open for 0% -> 1% of each run, Pallas kernels for 0% -> 20%
where the time goes in v1:
time: 143 us
  starting transfers between devices  55 us (38%)
  Pallas kernels  44.9 us (31%)
  waiting for transfers between devices  23.9 us (17%)
  blocking collectives  13.3 us (9%)
  local copies, waits for them, and re-layouts  4.75 us (3%)
    ppermute x27, starting transfers between devices, shifted(): return lax.ppermute(value, 'cd', permutation(dx, dz, dc))  55 us
    pallas_call x2, Pallas kernels, ladder(): pl.pallas_call(functools.partial(ladder_kernel, offset), out_shape=jax.Sh...  28.5 us
    ppermute x27, waiting for transfers between devices, shifted(): return lax.ppermute(value, 'cd', permutation(dx, dz, dc))  23.9 us
    pallas_call x12, Pallas kernels, hop(): pl.pallas_call(functools.partial(hop_kernel, n, group, units, len(msgs)),...  14.3 us
    all_gather x1, blocking collectives, body(): slab = lax.all_gather(amplitudes, 'ab', axis=0, tiled=True)  13.3 us
    unnamed x16, local copies, waits for them, and re-layouts  4.61 us
  transfers between devices with their start and end apart: 27, of which 9 were waited for; matrix products, arithmetic and copies ran while one was open for 1% of the time, Pallas kernels for 20%

profile of v1, /device:TPU:1, one launch (start us, length us, event | category | flops | bytes accessed | tf_op | source)
XLA Modules:
  0.0 142.8 jit_solution(7666211002952461785)
XLA Ops:
  0.0 3.2 %collective-permute-start.1 = (bf16[8,192,3072]{2,1,0:T(8,128)(2,1)}, bf16[8,192,3072]{2,1,0:T(8,128)(2,1)}, u32[]{:S(2)}, u32[]{:S(2)}) collective-permute-start(bf16[8,192,3072]{2,1,0:T(8,128)(2,1)} %v0_ref.3), channel_id=1, source_target_pairs={{0,1},{1,0},{2,3},{3,2},{4,5},{5,4},{6,7},{7,6},{8,9},{9,8},{10,11... | collective-permute-start | bytes 28311560 | tf_op jit(solution)/shard_map/ppermute | solution.py:34
  3.2 1.1 copy.6
  4.3 13.3 %all_gather.3 = bf16[2048,192]{1,0:T(8,128)(2,1)S(1)} all-gather(bf16[512,192]{1,0:T(8,128)(2,1)S(1)} %copy.6), channel_id=1, replica_groups=mesh['ab'=4,'cd'=64] {'ab'}, dimensions={0}, use_global_device_ids=true | all-gather | bytes 983040 | tf_op jit(solution)/shard_map/all_gather | solution.py:258
  17.7 2.3 %collective-permute-start = (bf16[1024,192]{1,0:T(8,128)(2,1)S(1)}, bf16[1024,192]{1,0:T(8,128)(2,1)S(1)}, u32[]{:S(2)}, u32[]{:S(2)}) collective-permute-start(bf16[1024,192]{1,0:T(8,128)(2,1)S(1)} %get-tuple-element.57), channel_id=1, source_target_pairs={{0,1},{1,0},{2,3},{3,2},{4,5},{5,4},{6,7},{7,6},{8,9},{9,8},{10,11... | collective-permute-start | bytes 1179656 | tf_op jit(solution)/shard_map/ppermute | solution.py:34
  20.1 1.5 %collective-permute-done.t1_ref = bf16[1024,192]{1,0:T(8,128)(2,1)S(1)} collective-permute-done((bf16[1024,192]{1,0:T(8,128)(2,1)S(1)}, bf16[1024,192]{1,0:T(8,128)(2,1)S(1)}, u32[]{:S(2)}, u32[]{:S(2)}) %collective-permute-start) | collective-permute-done | bytes 393248 | tf_op jit(solution)/shard_map/ppermute | solution.py:34
  21.5 0.7 copy-done.4
  22.2 13.8 %ladder.3.refs_0_.refs_1_ = f32[3072,512]{1,0:T(8,128)S(1)} custom-call(s32[3]{0:T(128)S(1)} %pad_add_fusion.meta, s32[8]{0:T(128)S(1)} %copy-done.4, bf16[1024,192]{1,0:T(8,128)(2,1)S(1)} %get-tuple-element.58.t0_ref, bf16[1024,192]{1,0:T(8,128)(2,1)S(1)} %collective-permute-done.t1_ref, bf16[8,192,3072]{2,1,0:T(8,128)(2,1)} %v0_ref.3, ...), custom_call_target="tpu_custom_call" | custom-call | flops 2415919104 | bytes 31457280 | tf_op jit(solution)/shard_map/ladder/pallas_call | solution.py:68
  36.1 0.9 hop.18
  37.1 4.0 %collective-permute-start.15 = (s16[208,512]{1,0:T(8,128)(2,1)S(1)}, s16[208,512]{1,0:T(8,128)(2,1)S(1)}, u32[]{:S(2)}, u32[]{:S(2)}) collective-permute-start(s16[208,512]{1,0:T(8,128)(2,1)S(1)} %get-tuple-element.44), channel_id=1, source_target_pairs={{0,14},{1,15},{2,0},{3,1},{4,2},{5,3},{6,4},{7,5},{8,6},{9,7},{10,... | collective-permute-start | bytes 638984 | tf_op jit(solution)/shard_map/ppermute | solution.py:34
  41.1 14.6 %ladder.2.refs_0_.refs_1_ = f32[3072,512]{1,0:T(8,128)S(1)} custom-call(s32[3]{0:T(128)S(1)} %pad_add_fusion.meta, s32[8]{0:T(128)S(1)} %copy-done.4, bf16[1024,192]{1,0:T(8,128)(2,1)S(1)} %get-tuple-element.58.t0_ref, bf16[1024,192]{1,0:T(8,128)(2,1)S(1)} %collective-permute-done.t1_ref, bf16[8,192,3072]{2,1,0:T(8,128)(2,1)} %v0_ref.3, ...), custom_call_target="tpu_custom_call" | custom-call | flops 2415919104 | bytes 31457280 | tf_op jit(solution)/shard_map/ladder/pallas_call | solution.py:68
  55.8 1.1 hop.12
  56.9 1.3 collective-permute-start.2
  58.2 1.5 %collective-permute-start.3 = (s16[400,512]{1,0:T(8,128)(2,1)S(1)}, s16[400,512]{1,0:T(8,128)(2,1)S(1)}, u32[]{:S(2)}, u32[]{:S(2)}) collective-permute-start(s16[400,512]{1,0:T(8,128)(2,1)S(1)} %get-tuple-element.32), channel_id=1, source_target_pairs={{0,48},{1,49},{2,50},{3,51},{4,52},{5,53},{6,54},{7,55},{8,56},{9,... | collective-permute-start | bytes 1228808 | tf_op jit(solution)/shard_map/ppermute | solution.py:34
  59.6 1.4 hop.19
  61.2 2.7 %collective-permute-start.17 = (s16[400,512]{1,0:T(8,128)(2,1)S(1)}, s16[400,512]{1,0:T(8,128)(2,1)S(1)}, u32[]{:S(2)}, u32[]{:S(2)}) collective-permute-start(s16[400,512]{1,0:T(8,128)(2,1)S(1)} %get-tuple-element.46), channel_id=1, source_target_pairs={{0,14},{1,15},{2,0},{3,1},{4,2},{5,3},{6,4},{7,5},{8,6},{9,7},{10,... | collective-permute-start | bytes 1228808 | tf_op jit(solution)/shard_map/ppermute | solution.py:34
  63.8 1.2 collective-permute-done.2.refs_2_
  65.0 2.1 %hop.13 = (s16[784,512]{1,0:T(8,128)(2,1)S(1)}, s16[784,512]{1,0:T(8,128)(2,1)S(1)}) custom-call(s32[3]{0:T(128)S(1)} %pad_add_fusion.meta, f32[3072,512]{1,0:T(8,128)S(1)} %ladder.2.refs_0_.refs_1_, f32[3072,512]{1,0:T(8,128)S(1)} %ladder.2.refs_0_.refs_1_, s16[400,512]{1,0:T(8,128)(2,1)S(1)} %collective-permute-done.2.refs_2_, ...), custom_call_target="tpu_custom_call" | custom-call | flops 7864320 | bytes 6291456 | tf_op jit(solution)/shard_map/hop/pallas_call | solution.py:147
  67.1 1.3 collective-permute-start.4
  68.4 1.5 %collective-permute-start.5 = (s16[784,512]{1,0:T(8,128)(2,1)S(1)}, s16[784,512]{1,0:T(8,128)(2,1)S(1)}, u32[]{:S(2)}, u32[]{:S(2)}) collective-permute-start(s16[784,512]{1,0:T(8,128)(2,1)S(1)} %get-tuple-element.34), channel_id=1, source_target_pairs={{0,48},{1,49},{2,50},{3,51},{4,52},{5,53},{6,54},{7,55},{8,56},{9,... | collective-permute-start | bytes 2408456 | tf_op jit(solution)/shard_map/ppermute | solution.py:34
  69.9 1.4 hop.20
  71.4 2.7 %collective-permute-start.19 = (s16[400,512]{1,0:T(8,128)(2,1)S(1)}, s16[400,512]{1,0:T(8,128)(2,1)S(1)}, u32[]{:S(2)}, u32[]{:S(2)}) collective-permute-start(s16[400,512]{1,0:T(8,128)(2,1)S(1)} %get-tuple-element.48), channel_id=1, source_target_pairs={{0,14},{1,15},{2,0},{3,1},{4,2},{5,3},{6,4},{7,5},{8,6},{9,7},{10,... | collective-permute-start | bytes 1228808 | tf_op jit(solution)/shard_map/ppermute | solution.py:34
  74.1 6.6 %collective-permute-done.18.refs_2_ = s16[400,512]{1,0:T(8,128)(2,1)S(1)} collective-permute-done((s16[400,512]{1,0:T(8,128)(2,1)S(1)}, s16[400,512]{1,0:T(8,128)(2,1)S(1)}, u32[]{:S(2)}, u32[]{:S(2)}) %collective-permute-start.18) | collective-permute-done | bytes 409632 | tf_op jit(solution)/shard_map/ppermute | solution.py:34
  80.7 1.4 hop.21
  82.7 2.6 %collective-permute-start.21 = (s16[400,512]{1,0:T(8,128)(2,1)S(1)}, s16[400,512]{1,0:T(8,128)(2,1)S(1)}, u32[]{:S(2)}, u32[]{:S(2)}) collective-permute-start(s16[400,512]{1,0:T(8,128)(2,1)S(1)} %get-tuple-element.50), channel_id=1, source_target_pairs={{0,14},{1,15},{2,0},{3,1},{4,2},{5,3},{6,4},{7,5},{8,6},{9,7},{10,... | collective-permute-start | bytes 1228808 | tf_op jit(solution)/shard_map/ppermute | solution.py:34
  85.3 0.7 hop.14
  86.0 2.7 %collective-permute-start.7 = (s16[64,512]{1,0:T(8,128)(2,1)S(1)}, s16[64,512]{1,0:T(8,128)(2,1)S(1)}, u32[]{:S(2)}, u32[]{:S(2)}) collective-permute-start(s16[64,512]{1,0:T(8,128)(2,1)S(1)} %get-tuple-element.36), channel_id=1, source_target_pairs={{0,14},{1,15},{2,0},{3,1},{4,2},{5,3},{6,4},{7,5},{8,6},{9,7},{10,... | collective-permute-start | bytes 196616 | tf_op jit(solution)/shard_map/ppermute | solution.py:34
  88.7 4.7 %collective-permute-done.6.refs_4_ = s16[64,512]{1,0:T(8,128)(2,1)S(1)} collective-permute-done((s16[64,512]{1,0:T(8,128)(2,1)S(1)}, s16[64,512]{1,0:T(8,128)(2,1)S(1)}, u32[]{:S(2)}, u32[]{:S(2)}) %collective-permute-start.6) | collective-permute-done | bytes 65568 | tf_op jit(solution)/shard_map/ppermute | solution.py:34
  93.4 0.9 hop.15
  94.3 2.5 %collective-permute-start.8 = (s16[112,512]{1,0:T(8,128)(2,1)S(1)}, s16[112,512]{1,0:T(8,128)(2,1)S(1)}, u32[]{:S(2)}, u32[]{:S(2)}) collective-permute-start(s16[112,512]{1,0:T(8,128)(2,1)S(1)} %get-tuple-element.37), channel_id=1, source_target_pairs={{0,2},{1,3},{2,4},{3,5},{4,6},{5,7},{6,8},{7,9},{8,10},{9,11},{10,... | collective-permute-start | bytes 344072 | tf_op jit(solution)/shard_map/ppermute | solution.py:34
  96.8 0.6 collective-permute-start.9
  97.4 3.7 %collective-permute-done.8.refs_4_ = s16[112,512]{1,0:T(8,128)(2,1)S(1)} collective-permute-done((s16[112,512]{1,0:T(8,128)(2,1)S(1)}, s16[112,512]{1,0:T(8,128)(2,1)S(1)}, u32[]{:S(2)}, u32[]{:S(2)}) %collective-permute-start.8) | collective-permute-done | bytes 114720 | tf_op jit(solution)/shard_map/ppermute | solution.py:34
  101.1 1.1 collective-permute-done.9.refs_5_
  102.2 0.9 hop.16
  103.1 1.5 %collective-permute-start.10 = (s16[112,512]{1,0:T(8,128)(2,1)S(1)}, s16[112,512]{1,0:T(8,128)(2,1)S(1)}, u32[]{:S(2)}, u32[]{:S(2)}) collective-permute-start(s16[112,512]{1,0:T(8,128)(2,1)S(1)} %get-tuple-element.39), channel_id=1, source_target_pairs={{0,2},{1,3},{2,4},{3,5},{4,6},{5,7},{6,8},{7,9},{8,10},{9,11},{10,... | collective-permute-start | bytes 344072 | tf_op jit(solution)/shard_map/ppermute | solution.py:34
  104.6 1.3 collective-permute-start.11
  105.8 0.7 hop.22
  106.7 2.6 %collective-permute-start.23 = (s16[64,512]{1,0:T(8,128)(2,1)S(1)}, s16[64,512]{1,0:T(8,128)(2,1)S(1)}, u32[]{:S(2)}, u32[]{:S(2)}) collective-permute-start(s16[64,512]{1,0:T(8,128)(2,1)S(1)} %get-tuple-element.52), channel_id=1, source_target_pairs={{0,48},{1,49},{2,50},{3,51},{4,52},{5,53},{6,54},{7,55},{8,56},{9,... | collective-permute-start | bytes 196616 | tf_op jit(solution)/shard_map/ppermute | solution.py:34
  109.3 1.9 %collective-permute-done.22.refs_4_ = s16[64,512]{1,0:T(8,128)(2,1)S(1)} collective-permute-done((s16[64,512]{1,0:T(8,128)(2,1)S(1)}, s16[64,512]{1,0:T(8,128)(2,1)S(1)}, u32[]{:S(2)}, u32[]{:S(2)}) %collective-permute-start.22) | collective-permute-done | bytes 65568 | tf_op jit(solution)/shard_map/ppermute | solution.py:34
  111.2 1.4 hop.23
  113.1 2.2 %collective-permute-start.25 = (s16[112,512]{1,0:T(8,128)(2,1)S(1)}, s16[112,512]{1,0:T(8,128)(2,1)S(1)}, u32[]{:S(2)}, u32[]{:S(2)}) collective-permute-start(s16[112,512]{1,0:T(8,128)(2,1)S(1)} %get-tuple-element.54), channel_id=1, source_target_pairs={{0,48},{1,49},{2,50},{3,51},{4,52},{5,53},{6,54},{7,55},{8,56},{9,... | collective-permute-start | bytes 344072 | tf_op jit(solution)/shard_map/ppermute | solution.py:34
  115.3 1.5 %hop.17 = (s16[112,512]{1,0:T(8,128)(2,1)}, s16[112,512]{1,0:T(8,128)(2,1)}) custom-call(s32[3]{0:T(128)S(1)} %pad_add_fusion.meta, f32[3072,512]{1,0:T(8,128)S(1)} %ladder.2.refs_0_.refs_1_, f32[3072,512]{1,0:T(8,128)S(1)} %ladder.2.refs_0_.refs_1_, s16[784,512]{1,0:T(8,128)(2,1)S(1)} %collective-permute-done.4.refs_2_, ...), custom_call_target="tpu_custom_call" | custom-call | flops 983040 | bytes 786432 | tf_op jit(solution)/shard_map/hop/pallas_call | solution.py:147
  116.8 2.7 %collective-permute-start.13 = (s16[112,512]{1,0:T(8,128)(2,1)}, s16[112,512]{1,0:T(8,128)(2,1)S(1)}, u32[]{:S(2)}, u32[]{:S(2)}) collective-permute-start(s16[112,512]{1,0:T(8,128)(2,1)} %get-tuple-element.42), channel_id=1, source_target_pairs={{0,14},{1,15},{2,0},{3,1},{4,2},{5,3},{6,4},{7,5},{8,6},{9,7},{10,... | collective-permute-start | bytes 344072 | tf_op jit(solution)/shard_map/ppermute | solution.py:34
  119.7 2.2 %collective-permute-done.12.refs_4_ = s16[112,512]{1,0:T(8,128)(2,1)S(1)} collective-permute-done((s16[112,512]{1,0:T(8,128)(2,1)}, s16[112,512]{1,0:T(8,128)(2,1)S(1)}, u32[]{:S(2)}, u32[]{:S(2)}) %collective-permute-start.12) | collective-permute-done | bytes 114720 | tf_op jit(solution)/shard_map/ppermute | solution.py:34
  121.9 2.8 %copy-done.3 = f32[3072,512]{1,0:T(8,128)S(1)} copy-done((f32[3072,512]{1,0:T(8,128)S(1)}, f32[3072,512]{1,0:T(8,128)}, u32[]{:S(2)}) %copy-start.3) | copy-done | bytes 6291480
  124.7 2.1 %last.1 = (bf16[48,1024]{1,0:T(8,128)(2,1)S(1)}, bf16[48,1024]{1,0:T(8,128)(2,1)S(1)}) custom-call(s32[3]{0:T(128)S(1)} %pad_add_fusion.meta, s32[8]{0:T(128)S(1)} %copy-done.5, f32[3072,512]{1,0:T(8,128)S(1)} %copy-done.3, f32[3072,512]{1,0:T(8,128)} %copy-done.1, s16[784,512]{1,0:T(8,128)(2,1)S(1)} %collective-permute-done.4.refs_2_, ...), custom_call_target="tpu_custom_call" | custom-call | tf_op jit(solution)/shard_map/last/pallas_call | solution.py:238
  126.8 14.3 %collective-permute-start.26 = (bf16[48,1024]{1,0:T(8,128)(2,1)S(1)}, bf16[48,1024]{1,0:T(8,128)(2,1)S(1)}, u32[]{:S(2)}, u32[]{:S(2)}) collective-permute-start(bf16[48,1024]{1,0:T(8,128)(2,1)S(1)} %get-tuple-element.56), channel_id=1, source_target_pairs={{0,1},{1,0},{2,3},{3,2},{4,5},{5,4},{6,7},{7,6},{8,9},{9,8},{10,11... | collective-permute-start | bytes 294920 | tf_op jit(solution)/shard_map/ppermute | solution.py:34
  141.1 0.9 collective-permute-done.26
  142.1 0.7 maximum_bitcast_fusion
  (44 shorter events, 1.9 us)
Async XLA Ops:
  0.0 119.5 %copy-start = (f32[8,12288]{1,0:T(8,128)S(1)}, f32[8,12288]{1,0:T(8,128)}, u32[]{:S(2)}) copy-start(f32[8,12288]{1,0:T(8,128)} %param.9) | copy-start | bytes 1179652
  0.0 21.5 %collective-permute-start.1 = (bf16[8,192,3072]{2,1,0:T(8,128)(2,1)}, bf16[8,192,3072]{2,1,0:T(8,128)(2,1)}, u32[]{:S(2)}, u32[]{:S(2)}) collective-permute-start(bf16[8,192,3072]{2,1,0:T(8,128)(2,1)} %v0_ref.3), channel_id=1, source_target_pairs={{0,1},{1,0},{2,3},{3,2},{4,5},{5,4},{6,7},{7,6},{8,9},{9,8},{10,11... | collective-permute-start | bytes 28311560 | tf_op jit(solution)/shard_map/ppermute | solution.py:34
  17.7 3.9 %collective-permute-start = (bf16[1024,192]{1,0:T(8,128)(2,1)S(1)}, bf16[1024,192]{1,0:T(8,128)(2,1)S(1)}, u32[]{:S(2)}, u32[]{:S(2)}) collective-permute-start(bf16[1024,192]{1,0:T(8,128)(2,1)S(1)} %get-tuple-element.57), channel_id=1, source_target_pairs={{0,1},{1,0},{2,3},{3,2},{4,5},{5,4},{6,7},{7,6},{8,9},{9,8},{10,11... | collective-permute-start | bytes 1179656 | tf_op jit(solution)/shard_map/ppermute | solution.py:34
  21.5 0.7 copy-start.4
  36.1 75.2 %copy-start.1 = (f32[3072,512]{1,0:T(8,128)}, f32[3072,512]{1,0:T(8,128)S(1)}, u32[]{:S(2)}) copy-start(f32[3072,512]{1,0:T(8,128)S(1)} %ladder.3.refs_0_.refs_1_) | copy-start | bytes 18874372
  36.9 22.7 %collective-permute-start.14 = (s16[208,512]{1,0:T(8,128)(2,1)S(1)}, s16[208,512]{1,0:T(8,128)(2,1)S(1)}, u32[]{:S(2)}, u32[]{:S(2)}) collective-permute-start(s16[208,512]{1,0:T(8,128)(2,1)S(1)} %get-tuple-element.43), channel_id=1, source_target_pairs={{0,2},{1,3},{2,4},{3,5},{4,6},{5,7},{6,8},{7,9},{8,10},{9,11},{10,... | collective-permute-start | bytes 638984 | tf_op jit(solution)/shard_map/ppermute | solution.py:34
  37.1 22.5 %collective-permute-start.15 = (s16[208,512]{1,0:T(8,128)(2,1)S(1)}, s16[208,512]{1,0:T(8,128)(2,1)S(1)}, u32[]{:S(2)}, u32[]{:S(2)}) collective-permute-start(s16[208,512]{1,0:T(8,128)(2,1)S(1)} %get-tuple-element.44), channel_id=1, source_target_pairs={{0,14},{1,15},{2,0},{3,1},{4,2},{5,3},{6,4},{7,5},{8,6},{9,7},{10,... | collective-permute-start | bytes 638984 | tf_op jit(solution)/shard_map/ppermute | solution.py:34
  55.8 59.5 %copy-start.2 = (f32[3072,512]{1,0:T(8,128)}, f32[3072,512]{1,0:T(8,128)S(1)}, u32[]{:S(2)}) copy-start(f32[3072,512]{1,0:T(8,128)S(1)} %ladder.2.refs_0_.refs_1_) | copy-start | bytes 18874372
  56.9 8.1 %collective-permute-start.2 = (s16[400,512]{1,0:T(8,128)(2,1)S(1)}, s16[400,512]{1,0:T(8,128)(2,1)S(1)}, u32[]{:S(2)}, u32[]{:S(2)}) collective-permute-start(s16[400,512]{1,0:T(8,128)(2,1)S(1)} %get-tuple-element.31), channel_id=1, source_target_pairs={{0,16},{1,17},{2,18},{3,19},{4,20},{5,21},{6,22},{7,23},{8,24},{9,... | collective-permute-start | bytes 1228808 | tf_op jit(solution)/shard_map/ppermute | solution.py:34
  58.2 6.8 %collective-permute-start.3 = (s16[400,512]{1,0:T(8,128)(2,1)S(1)}, s16[400,512]{1,0:T(8,128)(2,1)S(1)}, u32[]{:S(2)}, u32[]{:S(2)}) collective-permute-start(s16[400,512]{1,0:T(8,128)(2,1)S(1)} %get-tuple-element.32), channel_id=1, source_target_pairs={{0,48},{1,49},{2,50},{3,51},{4,52},{5,53},{6,54},{7,55},{8,56},{9,... | collective-permute-start | bytes 1228808 | tf_op jit(solution)/shard_map/ppermute | solution.py:34
  61.1 8.9 %collective-permute-start.16 = (s16[400,512]{1,0:T(8,128)(2,1)S(1)}, s16[400,512]{1,0:T(8,128)(2,1)S(1)}, u32[]{:S(2)}, u32[]{:S(2)}) collective-permute-start(s16[400,512]{1,0:T(8,128)(2,1)S(1)} %get-tuple-element.45), channel_id=1, source_target_pairs={{0,2},{1,3},{2,4},{3,5},{4,6},{5,7},{6,8},{7,9},{8,10},{9,11},{10,... | collective-permute-start | bytes 1228808 | tf_op jit(solution)/shard_map/ppermute | solution.py:34
  61.2 8.8 %collective-permute-start.17 = (s16[400,512]{1,0:T(8,128)(2,1)S(1)}, s16[400,512]{1,0:T(8,128)(2,1)S(1)}, u32[]{:S(2)}, u32[]{:S(2)}) collective-permute-start(s16[400,512]{1,0:T(8,128)(2,1)S(1)} %get-tuple-element.46), channel_id=1, source_target_pairs={{0,14},{1,15},{2,0},{3,1},{4,2},{5,3},{6,4},{7,5},{8,6},{9,7},{10,... | collective-permute-start | bytes 1228808 | tf_op jit(solution)/shard_map/ppermute | solution.py:34
  67.1 18.2 %collective-permute-start.4 = (s16[784,512]{1,0:T(8,128)(2,1)S(1)}, s16[784,512]{1,0:T(8,128)(2,1)S(1)}, u32[]{:S(2)}, u32[]{:S(2)}) collective-permute-start(s16[784,512]{1,0:T(8,128)(2,1)S(1)} %get-tuple-element.33), channel_id=1, source_target_pairs={{0,16},{1,17},{2,18},{3,19},{4,20},{5,21},{6,22},{7,23},{8,24},{9,... | collective-permute-start | bytes 2408456 | tf_op jit(solution)/shard_map/ppermute | solution.py:34
  68.4 16.9 %collective-permute-start.5 = (s16[784,512]{1,0:T(8,128)(2,1)S(1)}, s16[784,512]{1,0:T(8,128)(2,1)S(1)}, u32[]{:S(2)}, u32[]{:S(2)}) collective-permute-start(s16[784,512]{1,0:T(8,128)(2,1)S(1)} %get-tuple-element.34), channel_id=1, source_target_pairs={{0,48},{1,49},{2,50},{3,51},{4,52},{5,53},{6,54},{7,55},{8,56},{9,... | collective-permute-start | bytes 2408456 | tf_op jit(solution)/shard_map/ppermute | solution.py:34
  71.3 9.4 %collective-permute-start.18 = (s16[400,512]{1,0:T(8,128)(2,1)S(1)}, s16[400,512]{1,0:T(8,128)(2,1)S(1)}, u32[]{:S(2)}, u32[]{:S(2)}) collective-permute-start(s16[400,512]{1,0:T(8,128)(2,1)S(1)} %get-tuple-element.47), channel_id=1, source_target_pairs={{0,2},{1,3},{2,4},{3,5},{4,6},{5,7},{6,8},{7,9},{8,10},{9,11},{10,... | collective-permute-start | bytes 1228808 | tf_op jit(solution)/shard_map/ppermute | solution.py:34
  71.4 9.3 %collective-permute-start.19 = (s16[400,512]{1,0:T(8,128)(2,1)S(1)}, s16[400,512]{1,0:T(8,128)(2,1)S(1)}, u32[]{:S(2)}, u32[]{:S(2)}) collective-permute-start(s16[400,512]{1,0:T(8,128)(2,1)S(1)} %get-tuple-element.48), channel_id=1, source_target_pairs={{0,14},{1,15},{2,0},{3,1},{4,2},{5,3},{6,4},{7,5},{8,6},{9,7},{10,... | collective-permute-start | bytes 1228808 | tf_op jit(solution)/shard_map/ppermute | solution.py:34
  82.1 23.7 %collective-permute-start.20 = (s16[400,512]{1,0:T(8,128)(2,1)S(1)}, s16[400,512]{1,0:T(8,128)(2,1)S(1)}, u32[]{:S(2)}, u32[]{:S(2)}) collective-permute-start(s16[400,512]{1,0:T(8,128)(2,1)S(1)} %get-tuple-element.49), channel_id=1, source_target_pairs={{0,2},{1,3},{2,4},{3,5},{4,6},{5,7},{6,8},{7,9},{8,10},{9,11},{10,... | collective-permute-start | bytes 1228808 | tf_op jit(solution)/shard_map/ppermute | solution.py:34
  82.7 23.2 %collective-permute-start.21 = (s16[400,512]{1,0:T(8,128)(2,1)S(1)}, s16[400,512]{1,0:T(8,128)(2,1)S(1)}, u32[]{:S(2)}, u32[]{:S(2)}) collective-permute-start(s16[400,512]{1,0:T(8,128)(2,1)S(1)} %get-tuple-element.50), channel_id=1, source_target_pairs={{0,14},{1,15},{2,0},{3,1},{4,2},{5,3},{6,4},{7,5},{8,6},{9,7},{10,... | collective-permute-start | bytes 1228808 | tf_op jit(solution)/shard_map/ppermute | solution.py:34
  86.0 7.5 %collective-permute-start.6 = (s16[64,512]{1,0:T(8,128)(2,1)S(1)}, s16[64,512]{1,0:T(8,128)(2,1)S(1)}, u32[]{:S(2)}, u32[]{:S(2)}) collective-permute-start(s16[64,512]{1,0:T(8,128)(2,1)S(1)} %get-tuple-element.35), channel_id=1, source_target_pairs={{0,2},{1,3},{2,4},{3,5},{4,6},{5,7},{6,8},{7,9},{8,10},{9,11},{10,... | collective-permute-start | bytes 196616 | tf_op jit(solution)/shard_map/ppermute | solution.py:34
  86.0 7.4 %collective-permute-start.7 = (s16[64,512]{1,0:T(8,128)(2,1)S(1)}, s16[64,512]{1,0:T(8,128)(2,1)S(1)}, u32[]{:S(2)}, u32[]{:S(2)}) collective-permute-start(s16[64,512]{1,0:T(8,128)(2,1)S(1)} %get-tuple-element.36), channel_id=1, source_target_pairs={{0,14},{1,15},{2,0},{3,1},{4,2},{5,3},{6,4},{7,5},{8,6},{9,7},{10,... | collective-permute-start | bytes 196616 | tf_op jit(solution)/shard_map/ppermute | solution.py:34
  94.3 6.8 %collective-permute-start.8 = (s16[112,512]{1,0:T(8,128)(2,1)S(1)}, s16[112,512]{1,0:T(8,128)(2,1)S(1)}, u32[]{:S(2)}, u32[]{:S(2)}) collective-permute-start(s16[112,512]{1,0:T(8,128)(2,1)S(1)} %get-tuple-element.37), channel_id=1, source_target_pairs={{0,2},{1,3},{2,4},{3,5},{4,6},{5,7},{6,8},{7,9},{8,10},{9,11},{10,... | collective-permute-start | bytes 344072 | tf_op jit(solution)/shard_map/ppermute | solution.py:34
  96.8 5.4 %collective-permute-start.9 = (s16[112,512]{1,0:T(8,128)(2,1)S(1)}, s16[112,512]{1,0:T(8,128)(2,1)S(1)}, u32[]{:S(2)}, u32[]{:S(2)}) collective-permute-start(s16[112,512]{1,0:T(8,128)(2,1)S(1)} %get-tuple-element.38), channel_id=1, source_target_pairs={{0,14},{1,15},{2,0},{3,1},{4,2},{5,3},{6,4},{7,5},{8,6},{9,7},{10,... | collective-permute-start | bytes 344072 | tf_op jit(solution)/shard_map/ppermute | solution.py:34
  103.1 12.2 %collective-permute-start.10 = (s16[112,512]{1,0:T(8,128)(2,1)S(1)}, s16[112,512]{1,0:T(8,128)(2,1)S(1)}, u32[]{:S(2)}, u32[]{:S(2)}) collective-permute-start(s16[112,512]{1,0:T(8,128)(2,1)S(1)} %get-tuple-element.39), channel_id=1, source_target_pairs={{0,2},{1,3},{2,4},{3,5},{4,6},{5,7},{6,8},{7,9},{8,10},{9,11},{10,... | collective-permute-start | bytes 344072 | tf_op jit(solution)/shard_map/ppermute | solution.py:34
  104.6 10.7 %collective-permute-start.11 = (s16[112,512]{1,0:T(8,128)(2,1)S(1)}, s16[112,512]{1,0:T(8,128)(2,1)S(1)}, u32[]{:S(2)}, u32[]{:S(2)}) collective-permute-start(s16[112,512]{1,0:T(8,128)(2,1)S(1)} %get-tuple-element.40), channel_id=1, source_target_pairs={{0,14},{1,15},{2,0},{3,1},{4,2},{5,3},{6,4},{7,5},{8,6},{9,7},{10,... | collective-permute-start | bytes 344072 | tf_op jit(solution)/shard_map/ppermute | solution.py:34
  106.5 4.7 %collective-permute-start.22 = (s16[64,512]{1,0:T(8,128)(2,1)S(1)}, s16[64,512]{1,0:T(8,128)(2,1)S(1)}, u32[]{:S(2)}, u32[]{:S(2)}) collective-permute-start(s16[64,512]{1,0:T(8,128)(2,1)S(1)} %get-tuple-element.51), channel_id=1, source_target_pairs={{0,16},{1,17},{2,18},{3,19},{4,20},{5,21},{6,22},{7,23},{8,24},{9,... | collective-permute-start | bytes 196616 | tf_op jit(solution)/shard_map/ppermute | solution.py:34
  106.7 4.6 %collective-permute-start.23 = (s16[64,512]{1,0:T(8,128)(2,1)S(1)}, s16[64,512]{1,0:T(8,128)(2,1)S(1)}, u32[]{:S(2)}, u32[]{:S(2)}) collective-permute-start(s16[64,512]{1,0:T(8,128)(2,1)S(1)} %get-tuple-element.52), channel_id=1, source_target_pairs={{0,48},{1,49},{2,50},{3,51},{4,52},{5,53},{6,54},{7,55},{8,56},{9,... | collective-permute-start | bytes 196616 | tf_op jit(solution)/shard_map/ppermute | solution.py:34
  112.6 6.9 %copy-start.6 = (f32[2048]{0:T(1024)S(1)}, f32[2048]{0:T(1024)}, u32[]{:S(2)}) copy-start(f32[2048]{0:T(1024)} %param.8) | copy-start | bytes 24580
  112.6 9.3 %copy-start.5 = (s32[8]{0:T(128)S(1)}, s32[8]{0:T(128)}, u32[]{:S(2)}) copy-start(s32[8]{0:T(128)} %sizes.5) | copy-start | bytes 100
  112.6 7.1 %collective-permute-start.24 = (s16[112,512]{1,0:T(8,128)(2,1)}, s16[112,512]{1,0:T(8,128)(2,1)S(1)}, u32[]{:S(2)}, u32[]{:S(2)}) collective-permute-start(s16[112,512]{1,0:T(8,128)(2,1)} %get-tuple-element.53), channel_id=1, source_target_pairs={{0,16},{1,17},{2,18},{3,19},{4,20},{5,21},{6,22},{7,23},{8,24},{9,... | collective-permute-start | bytes 344072 | tf_op jit(solution)/shard_map/ppermute | solution.py:34
  113.1 6.6 %collective-permute-start.25 = (s16[112,512]{1,0:T(8,128)(2,1)S(1)}, s16[112,512]{1,0:T(8,128)(2,1)S(1)}, u32[]{:S(2)}, u32[]{:S(2)}) collective-permute-start(s16[112,512]{1,0:T(8,128)(2,1)S(1)} %get-tuple-element.54), channel_id=1, source_target_pairs={{0,48},{1,49},{2,50},{3,51},{4,52},{5,53},{6,54},{7,55},{8,56},{9,... | collective-permute-start | bytes 344072 | tf_op jit(solution)/shard_map/ppermute | solution.py:34
  116.8 5.1 %collective-permute-start.12 = (s16[112,512]{1,0:T(8,128)(2,1)}, s16[112,512]{1,0:T(8,128)(2,1)S(1)}, u32[]{:S(2)}, u32[]{:S(2)}) collective-permute-start(s16[112,512]{1,0:T(8,128)(2,1)} %get-tuple-element.41), channel_id=1, source_target_pairs={{0,2},{1,3},{2,4},{3,5},{4,6},{5,7},{6,8},{7,9},{8,10},{9,11},{10,... | collective-permute-start | bytes 344072 | tf_op jit(solution)/shard_map/ppermute | solution.py:34
  116.8 5.1 %collective-permute-start.13 = (s16[112,512]{1,0:T(8,128)(2,1)}, s16[112,512]{1,0:T(8,128)(2,1)S(1)}, u32[]{:S(2)}, u32[]{:S(2)}) collective-permute-start(s16[112,512]{1,0:T(8,128)(2,1)} %get-tuple-element.42), channel_id=1, source_target_pairs={{0,14},{1,15},{2,0},{3,1},{4,2},{5,3},{6,4},{7,5},{8,6},{9,7},{10,... | collective-permute-start | bytes 344072 | tf_op jit(solution)/shard_map/ppermute | solution.py:34
  121.9 2.8 %copy-start.3 = (f32[3072,512]{1,0:T(8,128)S(1)}, f32[3072,512]{1,0:T(8,128)}, u32[]{:S(2)}) copy-start(f32[3072,512]{1,0:T(8,128)} %copy-done.2) | copy-start | bytes 18874372
  126.8 15.3 %collective-permute-start.26 = (bf16[48,1024]{1,0:T(8,128)(2,1)S(1)}, bf16[48,1024]{1,0:T(8,128)(2,1)S(1)}, u32[]{:S(2)}, u32[]{:S(2)}) collective-permute-start(bf16[48,1024]{1,0:T(8,128)(2,1)S(1)} %get-tuple-element.56), channel_id=1, source_target_pairs={{0,1},{1,0},{2,3},{3,2},{4,5},{5,4},{6,7},{7,6},{8,9},{9,8},{10,11... | collective-permute-start | bytes 294920 | tf_op jit(solution)/shard_map/ppermute | solution.py:34
